TPU v7x, 32 devices: a whole 2x2x4 slice. The times are simulated.
32 devices in a mesh: half: 2 (over y), row: 4 (over x, core), col: 4 (over z).
Axes of the slice: x: 2, y: 2, z: 4, core: 2. Of those that a mesh axis runs over, the one named last changes fastest.
Arguments:
- front: bfloat16 [2, 16384, 16384], P('half', 'row', 'col'), may hold values from -6 to 6, as said below
- panel: bfloat16 [2, 16384, 1024], P('half', 'row', 'col'), may hold values from -2.5 to 2.5
- inverse_block: bfloat16 [2, 1024, 1024], P('half', None, 'col'), as said below
- child_maps: int32 [2, 16384], replicated, may hold values from 0 to 16383, as said below
- root_front: bfloat16 [16384, 16384], P(('half', 'row'), 'col'), may hold values from -6 to 6, as said below
Outputs:
- root_sum: float32 [16384, 16384], P(('half', 'row'), 'col')
Inputs may be any that keep to these rules, and one draw needn't show every extreme that they name: `child_maps`: each row is a permutation of the 16384 root indices. For each child, in every aligned block of 4096 positions, the k-th aligned run of 512 positions maps into the k-th aligned block of 2048 root indices. `inverse_block`: each matrix is lower triangular with a positive diagonal. `front`: each child's matrix is symmetric. `root_front`: the matrix is symmetric.
All inputs are finite; a program needn't handle non-finite values.
Results may differ from a plain program's by a relative error of at most 0.0041.
Values may be sent and summed in bfloat16 or wider, within the bound.
A program may use at most 256 MiB of HBM per device.

v0:
```python
import jax
import jax.numpy as jnp
from jax import lax
from jax.sharding import PartitionSpec as P


def spread(array, axis, root):
    mine = lax.axis_index(axis) == root
    return lax.psum(jnp.where(mine, array, jnp.zeros_like(array)), axis)


def contract(left, right):
    return lax.dot_general(
        left, right, (((1,), (1,)), ((), ())), preferred_element_type=jnp.float32
    )


def body(front, panel, inverse_block, child_maps, root_front):
    rows_count = lax.axis_size("row")
    cols_count = lax.axis_size("col")
    halves = lax.axis_size("half")
    half_idx = lax.axis_index("half")
    row_idx = lax.axis_index("row")
    col_idx = lax.axis_index("col")
    block_front = front[0]
    panel_part = panel[0]
    inverse_part = inverse_block[0]
    span_rows = block_front.shape[0]
    partial_lower = contract(panel_part, inverse_part)
    lower_rows = lax.psum(partial_lower, "col").astype(jnp.bfloat16)
    lower_cols = spread(lower_rows, "row", col_idx)
    update = contract(lower_rows, lower_cols)
    schur_block = (block_front.astype(jnp.float32) - update).astype(jnp.bfloat16)
    groups = halves * rows_count
    row_share = span_rows // groups
    col_share = span_rows // cols_count
    parcel = schur_block.reshape(groups, row_share, cols_count, col_share)
    arrived = lax.all_to_all(
        lax.all_to_all(parcel, ("half", "row"), split_axis=0, concat_axis=0, tiled=True),
        "col",
        split_axis=2,
        concat_axis=2,
        tiled=True,
    )
    target = half_idx * rows_count + row_idx
    root_rows = root_front.shape[0]
    root_cols = root_front.shape[1]
    block_maps = child_maps.reshape(halves, rows_count, span_rows)
    column_ids = jnp.arange(root_cols, dtype=jnp.int32)[None, :]
    summed = root_front.astype(jnp.float32)
    for child_idx in range(halves):
        arrival_rows = (
            lax.dynamic_slice_in_dim(
                block_maps[child_idx], target * row_share, row_share, 1
            ).reshape(-1)
            - target * root_rows
        )
        arrival_cols = (
            lax.dynamic_slice_in_dim(
                block_maps[child_idx], col_idx * col_share, col_share, 1
            ).reshape(-1)
            - col_idx * root_cols
        )
        place_rows = (
            jnp.zeros((root_rows,), jnp.int32)
            .at[arrival_rows]
            .set(jnp.arange(root_rows, dtype=jnp.int32))
        )
        portion = arrived[child_idx * rows_count : (child_idx + 1) * rows_count].reshape(
            root_rows, root_cols
        )
        rowed = jnp.take(portion, place_rows, axis=0)
        selector = (arrival_cols[:, None] == column_ids).astype(jnp.bfloat16)
        summed = summed + jnp.dot(rowed, selector, preferred_element_type=jnp.float32)
    global_rows = target * root_rows + jnp.arange(root_rows, dtype=jnp.int32)[:, None]
    global_cols = col_idx * root_cols + jnp.arange(root_cols, dtype=jnp.int32)[None, :]
    return jnp.where(global_rows >= global_cols, summed, jnp.zeros_like(summed))


def solution(mesh):
    return jax.shard_map(
        body,
        mesh=mesh,
        in_specs=(
            P("half", "row", "col"),
            P("half", "row", "col"),
            P("half", None, "col"),
            P(),
            P(("half", "row"), "col"),
        ),
        out_specs=P(("half", "row"), "col"),
        check_vma=False,
    )
```

profile of v0, /device:TPU:11, one launch (start us, length us, event | category | flops | bytes accessed | tf_op | source)
XLA Modules:
  0.0 2307.7 jit_solution(5506996143893493836)
XLA Ops:
  6.5 1.6 copy-done
  8.1 9.6 fusion.12
  17.7 553.7 %all-reduce.4 = bf16[4096,1024]{1,0:T(8,128)(2,1)} all-reduce(f32[4096,1024]{1,0:T(8,128)} %fusion.12), channel_id=1, replica_groups=mesh['half'=2,'row'=4,'col'=4] {'col'}, use_global_device_ids=true, to_apply=%region_0.0 | all-reduce | flops 4194304 | bytes 25165824 | tf_op jit(solution)/shard_map/psum | solution.py:30
  571.4 3.9 broadcast_select_fusion
  575.4 0.0 all-reduce.3.cloned.1.call-update
  575.4 159.8 %all-reduce.3.cloned.1.call-done = bf16[4096,1024]{1,0:T(8,128)(2,1)} async-done(((bf16[4096,1024]{1,0:T(8,128)(2,1)}), bf16[4096,1024]{1,0:T(8,128)(2,1)}) %all-reduce.3.cloned.1.call-update) | async-done | bytes 8388624 | tf_op jit(solution)/shard_map/psum | solution.py:9
  735.2 44.1 %fusion = bf16[4096,4096]{1,0:T(8,128)(2,1)} fusion(bf16[4096,1024]{1,0:T(8,128)(2,1)} %all-reduce.3.cloned.1.call-done, bf16[1,4096,4096]{2,1,0:T(8,128)(2,1)} %param.7, bf16[4096,1024]{1,0:T(8,128)(2,1)} %all-reduce.4), kind=kOutput, calls=%fused_computation.5 | convolution fusion | flops 34410070016 | bytes 83886080 | tf_op jit(solution)/shard_map/dot_general | solution.py:13
  779.3 54.5 %reshape.91 = bf16[8,512,4,1024]{3,2,1,0:T(4,128)(2,1)} reshape(bf16[4096,4096]{1,0:T(8,128)(2,1)} %fusion) | data formatting | bytes 67108864 | tf_op jit(solution)/shard_map/reshape | solution.py:37
  833.9 22.7 copy.9
  856.5 374.6 %all_to_all.10 = bf16[8,512,4,1024]{3,1,2,0:T(8,128)(2,1)} all-to-all(bf16[8,512,4,1024]{3,1,2,0:T(8,128)(2,1)} %copy.9), channel_id=1, replica_groups=mesh['half'=2,'row'=4,'col'=4] {'half','row'}, dimensions={0} | all-to-all | bytes 67108864 | tf_op jit(solution)/shard_map/all_to_all | solution.py:39
  1231.1 23.2 %copy.10 = bf16[8,512,4,1024]{3,1,0,2:T(8,128)(2,1)} copy(bf16[8,512,4,1024]{3,1,2,0:T(8,128)(2,1)} %all_to_all.10) | data formatting | bytes 67108864 | tf_op jit(solution)/shard_map/all_to_all | solution.py:39
  1254.4 10.3 all-to-all-start.1
  1264.6 0.3 slice_reduce_fusion.1
  1265.2 8.0 scatter_custom_fusion.1
  1273.3 8.0 scatter_custom_fusion
  1281.3 0.6 iota_add_fusion.1
  1281.9 0.6 iota_add_fusion
  1282.5 0.6 compare_and_fusion
  1283.1 0.6 compare_and_fusion.1
  1283.7 11.6 iota_compare_fusion.12
  1295.3 11.5 iota_compare_fusion.13
  1306.8 676.6 %all-to-all-done.1 = bf16[8,512,4,1024]{3,1,0,2:T(8,128)(2,1)} async-done(((bf16[8,512,4,1024]{3,1,0,2:T(8,128)(2,1)}), bf16[8,512,4,1024]{3,1,0,2:T(8,128)(2,1)}, u32[]{:S(2)}, u32[]{:S(2)}) %all-to-all-start.1) | async-done | bytes 33554464 | tf_op jit(solution)/shard_map/all_to_all | solution.py:38
  1983.4 23.1 %fusion.23 = (bf16[4,512,4,1024]{3,1,0,2:T(8,128)(2,1)}, bf16[4,512,4,1024]{3,1,0,2:T(8,128)(2,1)}) fusion(bf16[8,512,4,1024]{3,1,0,2:T(8,128)(2,1)} %all-to-all-done.1), kind=kLoop, calls=%fused_computation.48 | loop fusion | bytes 67108864 | tf_op jit(solution)/shard_map/slice | solution.py:69
  2006.5 19.1 copy.12
  2025.7 10.4 copy.17
  2036.1 19.1 copy.11
  2055.2 10.3 copy.14
  2065.5 36.8 %gather_fusion.1 = bf16[2048,4096]{1,0:T(8,128)(2,1)} fusion(bf16[2048,4096]{1,0:T(8,128)(2,1)} %bitcast.41, s32[2048]{0:T(1024)S(1)} %fusion.16), kind=kCustom, calls=%fused_computation.1.clone | custom fusion | bytes 33562624 | tf_op jit(solution)/shard_map/jit(_take)/gather | solution.py:72
  2102.3 36.6 %gather_fusion = bf16[2048,4096]{1,0:T(8,128)(2,1)} fusion(bf16[2048,4096]{1,0:T(8,128)(2,1)} %bitcast.42, s32[2048]{0:T(1024)S(1)} %fusion.15), kind=kCustom, calls=%fused_computation.clone | custom fusion | bytes 33562624 | tf_op jit(solution)/shard_map/jit(_take)/gather | solution.py:72
  2138.9 77.6 %fusion.2 = f32[2048,4096]{1,0:T(8,128)} fusion(bf16[2048,4096]{1,0:T(8,128)(2,1)} %gather_fusion.1, pred[2048]{0:T(1024)(128)(4,1)S(1)} %copy-done.6, pred[4096,4096]{1,0:T(32,128)(4,1)} %iota_compare_fusion.12), kind=kOutput, calls=%fused_computation.9 | convolution fusion | flops 68727865344 | bytes 67110912 | tf_op jit(solution)/shard_map/dot_general | solution.py:74
  2216.6 0.0 copy-start.1
  2216.6 83.9 %add_select_fusion = f32[2048,4096]{1,0:T(8,128)} fusion(f32[2048,4096]{1,0:T(8,128)} %fusion.2, bf16[2048,4096]{1,0:T(8,128)(2,1)} %param.11, bf16[2048,4096]{1,0:T(8,128)(2,1)} %gather_fusion, s32[4096]{0:T(1024)S(1)} %copy-done.3, s32[2048]{0:T(1024)S(1)} %copy-done.4, pred[2048]{0:T(1024)(128)(4,1)S(1)} %copy-done.5, ...), kind=kOutput, calls=%fused_computation.10 | convolution fusion | flops 68769808384 | bytes 117467136 | tf_op jit(solution)/shard_map/dot_general | solution.py:74
  (27 shorter events, 0.2 us)
Async XLA Ops:
  6.5 1.6 copy-start
  6.5 728.7 %all-reduce.3.cloned.1.call-start = ((), (), s32[]{:S(2)}) async-start(), calls=%async_computation.2 | async-start | bytes 16777216 | tf_op jit(solution)/shard_map/psum | solution.py:9
  1254.4 10.3 copy-start.2
  1254.4 729.1 %all-to-all-start.1 = ((bf16[8,512,4,1024]{3,1,0,2:T(8,128)(2,1)}), bf16[8,512,4,1024]{3,1,0,2:T(8,128)(2,1)}, u32[]{:S(2)}, u32[]{:S(2)}) async-start(bf16[8,512,4,1024]{3,1,0,2:T(8,128)(2,1)} %copy.10), calls=%async_computation.1 | async-start | bytes 67108864 | tf_op jit(solution)/shard_map/all_to_all | solution.py:38
  2102.3 36.6 %copy-start.6 = (pred[2048]{0:T(1024)(128)(4,1)S(1)}, pred[2048]{0:T(1024)(128)(4,1)}, u32[]{:S(2)}) copy-start(pred[2048]{0:T(1024)(128)(4,1)} %compare_and_fusion) | copy-start | bytes 6148
  2138.9 77.7 %copy-start.3 = (s32[4096]{0:T(1024)S(1)}, s32[4096]{0:T(1024)}, u32[]{:S(2)}) copy-start(s32[4096]{0:T(1024)} %iota_add_fusion) | copy-start | bytes 49156
  2138.9 77.7 %copy-start.4 = (s32[2048]{0:T(1024)S(1)}, s32[2048]{0:T(1024)}, u32[]{:S(2)}) copy-start(s32[2048]{0:T(1024)} %iota_add_fusion.1) | copy-start | bytes 24580
  2138.9 77.7 %copy-start.5 = (pred[2048]{0:T(1024)(128)(4,1)S(1)}, pred[2048]{0:T(1024)(128)(4,1)}, u32[]{:S(2)}) copy-start(pred[2048]{0:T(1024)(128)(4,1)} %compare_and_fusion.1) | copy-start | bytes 6148
  2216.6 83.9 %copy-start.1 = (bf16[1,4096,256]{2,1,0:T(8,128)(2,1)S(1)}, bf16[1,4096,256]{2,1,0:T(8,128)(2,1)}, u32[]{:S(2)}) copy-start(bf16[1,4096,256]{2,1,0:T(8,128)(2,1)} %param.8) | copy-start | bytes 6291460
Sparse Core Ops, SparseCore 0:
  575.5 159.6 all-reduce.2
where the time goes:
time: 2320 us; the launch traced here: 2310 us
  blocking collectives  928 us (40%)
  waiting for transfers between devices  836 us (36%)
  local copies, waits for them, and re-layouts  274 us (12%)
  matrix products  215 us (9%)
  other arithmetic  29.5 us (1%)
    all_to_all x1, waiting for transfers between devices, body(): lax.all_to_all(lax.all_to_all(parcel, ('half', 'row'), split_axis=0, conc...  677 us
    psum x1, blocking collectives, body(): lower_rows = lax.psum(partial_lower, 'col').astype(jnp.bfloat16)  554 us
    all_to_all x1, blocking collectives, body(): lax.all_to_all(parcel, ('half', 'row'), split_axis=0, concat_axis=0, tile...  375 us
    dot_general x2, matrix products, body(): jnp.dot(rowed, selector, preferred_element_type=jnp.float32)  161 us
    psum x1, waiting for transfers between devices, spread(): return lax.psum(jnp.where(mine, array, jnp.zeros_like(array)), axis)  160 us
    reshape x2, local copies, waits for them, and re-layouts, body(): parcel = schur_block.reshape(groups, row_share, cols_count, col_share)  77.2 us
    gather x2, local copies, waits for them, and re-layouts, body(): rowed = jnp.take(portion, place_rows, axis=0)  73.4 us
    slice x3, local copies, waits for them, and re-layouts, body(): arrived[child_idx * rows_count:(child_idx + 1) * rows_count]  61.4 us
  transfers between devices with their start and end apart: 2, of which 2 were waited for; matrix products, arithmetic and copies ran while one was open for 2% of the time, Pallas kernels for 0%

commit v1 on v0

v1 whole, which is shorter than its diff:
```python
import functools

import jax
import jax.numpy as jnp
from jax import lax
from jax.experimental import pallas as pl
from jax.experimental.pallas import tpu as pltpu
from jax.sharding import PartitionSpec as P

MESH = pl.DeviceIdType.MESH


def contract(left, right):
    return lax.dot_general(
        left, right, (((1,), (1,)), ((), ())), preferred_element_type=jnp.float32
    )


def column_factor(lower, n):
    axes = ("row", "col")
    row_idx = lax.axis_index("row")
    col_idx = lax.axis_index("col")
    half_rows = lower.shape[0] // 2
    top, bottom = lower[:half_rows], lower[half_rows:]
    partner = lax.ppermute(lower, axes, [(c * n + c, (c ^ 1) * n + c) for c in range(n)])
    part = None
    for k in range(1, n // 2):
        evens, odds = [], []
        for c in range(n):
            far = 2 * ((c // 2 + k) % (n // 2))
            evens.append((c * n + c, far * n + c))
            odds.append((c * n + c, (far + 1) * n + c))
        got_even = lax.ppermute(top, axes, evens)
        got_odd = lax.ppermute(bottom, axes, odds)
        got = jnp.where(row_idx % 2 == 0, got_even, got_odd)
        part = got if part is None else part + got
    other = lax.ppermute(part, "row", [(r, r ^ 1) for r in range(n)])
    even = row_idx % 2 == 0
    joined = jnp.concatenate(
        [jnp.where(even, part, other), jnp.where(even, other, part)], axis=0
    )
    near = jnp.where(row_idx == col_idx, lower, partner)
    return jnp.where(row_idx // 2 == col_idx // 2, near, joined)


def exchange_kernel(n, schur, arr_a, arr_b, send_sem, recv_sem, local_sem):
    total = 2 * n * n
    h = lax.axis_index("half")
    r = lax.axis_index("row")
    z = lax.axis_index("col")
    me = (h * n + r) * n + z
    rs = arr_a.shape[3]
    cs = arr_a.shape[4]

    def place(index):
        return index // (n * n), (index // n) % n, index % n

    barrier = pltpu.get_barrier_semaphore()

    @pl.loop(1, total)
    def _(step):
        ph, pr, pz = place(lax.rem(me + step, total))
        pl.semaphore_signal(barrier, inc=1, device_id=(ph, pr, pz), device_id_type=MESH)

    pl.semaphore_wait(barrier, total - 1)

    def visit(step, act):
        ph, pr, pz = place(lax.rem(me + step, total))
        t = ph * n + pr
        near = jnp.abs(z - pz)
        far = jnp.abs(r - pz)
        row_at = pl.multiple_of(t * rs, rs)
        col_at = pl.multiple_of(pz * cs, cs)

        def remote(src, dst, kind):
            act(
                pltpu.make_async_remote_copy(
                    src_ref=src,
                    dst_ref=dst,
                    send_sem=send_sem.at[step, kind],
                    recv_sem=recv_sem.at[h, r, z] if kind == 0 else recv_sem.at[h, z, r],
                    device_id=(ph, pr, pz),
                    device_id_type=MESH,
                )
            )

        for width, fits in ((cs, t > 2 * pz), (rs, t == 2 * pz)):

            @pl.when(fits & (near <= far))
            def _():
                remote(
                    schur.at[pl.ds(row_at, rs), pl.ds(col_at, width)],
                    arr_a.at[h, r, z, :, pl.ds(0, width)],
                    0,
                )

            @pl.when(fits & (near < far))
            def _():
                remote(
                    schur.at[pl.ds(col_at, width), pl.ds(row_at, rs)],
                    arr_b.at[h, z, r, pl.ds(0, width), :],
                    1,
                )

    @pl.loop(1, total)
    def _(step):
        visit(step, lambda copy: copy.start())

    my_t = h * n + r
    row_at = pl.multiple_of(my_t * rs, rs)
    col_at = pl.multiple_of(z * cs, cs)
    own_a = pltpu.make_async_copy(
        schur.at[pl.ds(row_at, rs), pl.ds(col_at, cs)], arr_a.at[h, r, z], local_sem.at[0]
    )
    own_b = pltpu.make_async_copy(
        schur.at[pl.ds(col_at, cs), pl.ds(row_at, rs)], arr_b.at[h, z, r], local_sem.at[1]
    )
    own_a.start()
    own_b.start()
    own_a.wait()
    own_b.wait()

    @pl.loop(1, total)
    def _(step):
        visit(step, lambda copy: copy.wait_send())

    @pl.loop(1, total)
    def _(step):
        sh, sr, sz = place(lax.rem(me + total - step, total))
        near = jnp.abs(sz - z)
        far = jnp.abs(sr - z)
        for width, fits in ((cs, my_t > 2 * z), (rs, my_t == 2 * z)):

            @pl.when(fits & (near <= far))
            def _():
                dst = arr_a.at[sh, sr, sz, :, pl.ds(0, width)]
                pltpu.make_async_copy(dst, dst, recv_sem.at[sh, sr, sz]).wait()

            @pl.when(fits & (near < far))
            def _():
                dst = arr_b.at[sh, sz, sr, pl.ds(0, width), :]
                pltpu.make_async_copy(dst, dst, recv_sem.at[sh, sz, sr]).wait()


def exchange(schur, n):
    rs = schur.shape[0] // (2 * n)
    cs = 2 * rs
    return pl.pallas_call(
        functools.partial(exchange_kernel, n),
        out_shape=(
            jax.ShapeDtypeStruct((2, n, n, rs, cs), schur.dtype),
            jax.ShapeDtypeStruct((2, n, n, cs, rs), schur.dtype),
        ),
        in_specs=[pl.BlockSpec(memory_space=pl.ANY)],
        out_specs=(pl.BlockSpec(memory_space=pl.ANY), pl.BlockSpec(memory_space=pl.ANY)),
        scratch_shapes=[
            pltpu.SemaphoreType.DMA((2 * n * n, 2)),
            pltpu.SemaphoreType.DMA((2, n, n)),
            pltpu.SemaphoreType.DMA((2,)),
        ],
        compiler_params=pltpu.CompilerParams(collective_id=0, has_side_effects=True),
    )(schur)


def assemble_kernel(n, row_map, col_map, arr_a, arr_b, root, out, square, rowed, sems):
    q = pl.program_id(0)
    j = pl.program_id(1)
    h_idx = lax.axis_index("half")
    r_idx = lax.axis_index("row")
    c_idx = lax.axis_index("col")
    t = h_idx * n + r_idx
    block = square.shape[1]
    rs = block // n
    tile = min(256, block)
    width = out.shape[1]
    needed = t >= 2 * c_idx + q

    def tiles(h, act):
        for b in range(n):
            for c in range(n):
                straight = jnp.abs(c - c_idx) <= jnp.abs(b - c_idx)
                dst = square.at[h, pl.ds(b * rs, rs), pl.ds(c * rs, rs)]
                act(b, c, straight, dst)

    @pl.when(needed & (j == 0))
    def _():
        def start(h, b, c, straight, dst):
            at = pl.multiple_of(q * rs, rs)

            @pl.when(straight)
            def _():
                pltpu.make_async_copy(
                    arr_a.at[h, b, c, :, pl.ds(at, rs)], dst, sems.at[h, b, c]
                ).start()

            @pl.when(jnp.logical_not(straight))
            def _():
                pltpu.make_async_copy(
                    arr_b.at[h, b, c, pl.ds(at, rs), :], dst, sems.at[h, b, c]
                ).start()

        def finish(h, b, c, straight, dst):
            pltpu.make_async_copy(
                arr_a.at[h, b, c, :, pl.ds(0, rs)], dst, sems.at[h, b, c]
            ).wait()

            @pl.when(jnp.logical_not(straight))
            def _():
                eye = (
                    lax.broadcasted_iota(jnp.int32, (rs, rs), 0)
                    == lax.broadcasted_iota(jnp.int32, (rs, rs), 1)
                ).astype(jnp.bfloat16)
                dst[...] = contract(eye, dst[...]).astype(jnp.bfloat16)

        for h in range(2):
            tiles(h, functools.partial(start, h))
        for h in range(2):
            tiles(h, functools.partial(finish, h))

            @pl.loop(0, block // tile)
            def _(i):
                at = pl.multiple_of(i * tile, tile)
                pick = (
                    lax.broadcasted_iota(jnp.int32, (tile, block), 0) + at
                    == row_map[h : h + 1, :]
                ).astype(jnp.bfloat16)
                rowed[h, pl.ds(at, tile), :] = jnp.dot(
                    pick, square[h], preferred_element_type=jnp.float32
                ).astype(jnp.bfloat16)

    @pl.when(needed)
    def _():
        ids = lax.broadcasted_iota(jnp.int32, (block, width), 1) + j * width
        picks = [
            (col_map[0, h, :, :] == ids).astype(jnp.bfloat16) for h in range(2)
        ]
        first_row = t * block
        first_col = (2 * c_idx + q) * block + j * width
        for i in range(block // tile):
            rows = pl.ds(i * tile, tile)
            value = root[rows, :].astype(jnp.float32)
            for h in range(2):
                value = value + jnp.dot(
                    rowed[h, rows, :], picks[h], preferred_element_type=jnp.float32
                )
            row_ids = lax.broadcasted_iota(jnp.int32, (tile, width), 0) + (
                first_row + i * tile
            )
            col_ids = lax.broadcasted_iota(jnp.int32, (tile, width), 1) + first_col
            out[rows, :] = jnp.where(row_ids >= col_ids, value, 0.0)

    @pl.when(jnp.logical_not(needed))
    def _():
        out[...] = jnp.zeros_like(out)


def assemble(row_map, col_map, arr_a, arr_b, root_front, n):
    block = root_front.shape[0]
    width = min(256, block)
    steps = block // width
    return pl.pallas_call(
        functools.partial(assemble_kernel, n),
        grid=(2, steps),
        out_shape=jax.ShapeDtypeStruct(root_front.shape, jnp.float32),
        in_specs=[
            pl.BlockSpec((2, block), lambda q, j: (0, 0)),
            pl.BlockSpec((1, 2, block, 1), lambda q, j: (q, 0, 0, 0)),
            pl.BlockSpec(memory_space=pl.ANY),
            pl.BlockSpec(memory_space=pl.ANY),
            pl.BlockSpec((block, width), lambda q, j: (0, q * steps + j)),
        ],
        out_specs=pl.BlockSpec((block, width), lambda q, j: (0, q * steps + j)),
        scratch_shapes=[
            pltpu.VMEM((2, block, block), jnp.bfloat16),
            pltpu.VMEM((2, block, block), jnp.bfloat16),
            pltpu.SemaphoreType.DMA((2, n, n)),
        ],
        compiler_params=pltpu.CompilerParams(vmem_limit_bytes=58 * 1024 * 1024),
    )(row_map, col_map, arr_a, arr_b, root_front)


def body(front, panel, inverse_block, child_maps, root_front):
    n = lax.axis_size("row")
    halves = lax.axis_size("half")
    target = lax.axis_index("half") * n + lax.axis_index("row")
    col_idx = lax.axis_index("col")
    block_front = front[0]
    span = block_front.shape[0]
    share = span // (halves * n)
    block = root_front.shape[0]

    full_panel = lax.all_gather(panel[0], "col", axis=1, tiled=True)
    full_inverse = lax.all_gather(inverse_block[0], "col", axis=1, tiled=True)
    lower_rows = contract(full_panel, full_inverse).astype(jnp.bfloat16)
    lower_cols = column_factor(lower_rows, n)
    update = contract(lower_rows, lower_cols)
    schur_block = (block_front.astype(jnp.float32) - update).astype(jnp.bfloat16)
    arr_a, arr_b = exchange(schur_block, n)

    runs = child_maps.reshape(halves, n, halves * n, share)

    def local_ids(run):
        picked = lax.dynamic_index_in_dim(runs, run, axis=2, keepdims=False)
        return picked.reshape(halves, n * share) - run * block

    row_map = local_ids(target)
    col_map = jnp.stack([local_ids(2 * col_idx), local_ids(2 * col_idx + 1)])
    return assemble(row_map, col_map[..., None], arr_a, arr_b, root_front, n)


def solution(mesh):
    return jax.shard_map(
        body,
        mesh=mesh,
        in_specs=(
            P("half", "row", "col"),
            P("half", "row", "col"),
            P("half", None, "col"),
            P(),
            P(("half", "row"), "col"),
        ),
        out_specs=P(("half", "row"), "col"),
        check_vma=False,
    )
```

time: 2320 us -> 1250 us (0.54)
  blocking collectives: 928 us -> 0 us
  Pallas kernels: 0 us -> 858 us
  waiting for transfers between devices: 836 us -> 287 us
  local copies, waits for them, and re-layouts: 274 us -> 9.39 us
  matrix products: 215 us -> 63.4 us
    pallas_call x0 -> x2, Pallas kernels: none -> 858 us  [the longest x1 690 us: exchange(): pl.pallas_call(functools.partial(exchange_kernel, n), out_shape=(jax.Shap...]
    all_to_all x1 -> x0, waiting for transfers between devices: 677 us -> none  [body(): lax.all_to_all(lax.all_to_all(parcel, ('half', 'row'), split_axis=0, conc...]
    psum x1 -> x0, blocking collectives: 554 us -> none  [body(): lower_rows = lax.psum(partial_lower, 'col').astype(jnp.bfloat16)]
    all_to_all x1 -> x0, blocking collectives: 375 us -> none  [body(): lax.all_to_all(parcel, ('half', 'row'), split_axis=0, concat_axis=0, tile...]
    all_gather x0 -> x2, waiting for transfers between devices: none -> 195 us  [the longest x1 149 us: body(): full_panel = lax.all_gather(panel[0], 'col', axis=1, tiled=True)]
    dot_general x2 -> x0, matrix products: 161 us -> none  [body(): jnp.dot(rowed, selector, preferred_element_type=jnp.float32)]
    psum x1 -> x0, waiting for transfers between devices: 160 us -> none  [spread(): return lax.psum(jnp.where(mine, array, jnp.zeros_like(array)), axis)]
    ppermute x0 -> x4, waiting for transfers between devices: none -> 91.2 us  [the longest x1 87.2 us: column_factor(): got_odd = lax.ppermute(bottom, axes, odds)]
  transfers between devices with their start and end apart: 2 -> 6, of which waited for: 2 -> 4; matrix products, arithmetic and copies ran while one was open for 2% -> 1% of each run, Pallas kernels for 0% -> 0%
where the time goes in v1:
time: 1250 us
  Pallas kernels  858 us (69%)
  waiting for transfers between devices  287 us (23%)
  matrix products  63.4 us (5%)
  between operations  13.5 us (1%)
    pallas_call x1, Pallas kernels, exchange(): pl.pallas_call(functools.partial(exchange_kernel, n), out_shape=(jax.Shap...  690 us
    pallas_call x1, Pallas kernels, assemble(): pl.pallas_call(functools.partial(assemble_kernel, n), grid=(2, steps), ou...  168 us
    all_gather x1, waiting for transfers between devices, body(): full_panel = lax.all_gather(panel[0], 'col', axis=1, tiled=True)  149 us
    ppermute x1, waiting for transfers between devices, column_factor(): got_odd = lax.ppermute(bottom, axes, odds)  87.2 us
    dot_general x2, matrix products, contract(): lax.dot_general(left, right, (((1,), (1,)), ((), ())), preferred_element_...  63.4 us
    all_gather x1, waiting for transfers between devices, body(): full_inverse = lax.all_gather(inverse_block[0], 'col', axis=1, tiled=True)  45.6 us
  transfers between devices with their start and end apart: 6, of which 4 were waited for; matrix products, arithmetic and copies ran while one was open for 1% of the time, Pallas kernels for 0%

profile of v1, /device:TPU:11, one launch (start us, length us, event | category | flops | bytes accessed | tf_op | source)
XLA Modules:
  0.0 1247.9 jit_solution(13455379289108429118)
XLA Ops:
  6.5 0.0 all-gather.7.cloned.1.call-start
  6.5 0.7 all-gather.7.cloned.1.call-update
  7.3 0.0 all-gather.5.cloned.1.call-start
  7.3 0.7 all-gather.5.cloned.1.call-update
  8.0 45.6 %all-gather.7.cloned.1.call-done = bf16[1,1024,1024]{2,1,0:T(8,128)(2,1)} async-done(((bf16[1,1024,256]{2,1,0:T(8,128)(2,1)}), bf16[1,1024,1024]{2,1,0:T(8,128)(2,1)}) %all-gather.7.cloned.1.call-update) | async-done | bytes 2097168 | tf_op jit(solution)/shard_map/all_gather | solution.py:293
  53.6 148.9 %all-gather.5.cloned.1.call-done = bf16[1,4096,1024]{2,1,0:T(8,128)(2,1)} async-done(((bf16[1,4096,256]{2,1,0:T(8,128)(2,1)}), bf16[1,4096,1024]{2,1,0:T(8,128)(2,1)}) %all-gather.5.cloned.1.call-update) | async-done | bytes 8388624 | tf_op jit(solution)/shard_map/all_gather | solution.py:292
  202.5 14.9 %fusion.8 = bf16[4096,1024]{1,0:T(8,128)(2,1)} fusion(bf16[1,4096,1024]{2,1,0:T(8,128)(2,1)} %all-gather.5.cloned.1.call-done, bf16[1,1024,1024]{2,1,0:T(8,128)(2,1)} %all-gather.7.cloned.1.call-done), kind=kOutput, calls=%fused_computation.10 | convolution fusion | flops 8594128896 | bytes 18874368 | tf_op jit(solution)/shard_map/dot_general | solution.py:14
  217.5 6.0 fusion.14
  223.5 0.0 copy-start
  223.5 2.8 collective-permute-start.1
  226.3 1.3 collective-permute-start.2
  227.6 3.9 collective-permute-start
  231.5 0.0 collective-permute-done.1
  231.5 87.2 %collective-permute-done.2 = bf16[2048,1024]{1,0:T(8,128)(2,1)} collective-permute-done((bf16[2048,1024]{1,0:T(8,128)(2,1)}, bf16[2048,1024]{1,0:T(8,128)(2,1)}, u32[]{:S(2)}, u32[]{:S(2)}) %collective-permute-start.2) | collective-permute-done | bytes 4194336 | tf_op jit(solution)/shard_map/ppermute | solution.py:34
  318.7 4.6 broadcast_select_fusion.2
  323.3 0.0 collective-permute-start.3
  323.3 0.0 copy-done
  323.4 0.1 subtract_reduce_fusion.1
  323.6 2.7 copy.10.col_map
  326.2 0.6 copy.13
  326.9 4.0 collective-permute-done.3
  330.8 3.8 broadcast_select_fusion.1
  334.6 0.0 collective-permute-done
  334.6 48.4 %fusion.schur = bf16[4096,4096]{1,0:T(8,128)(2,1)} fusion(bf16[4096,1024]{1,0:T(8,128)(2,1)} %fusion.8, bf16[1,4096,4096]{2,1,0:T(8,128)(2,1)} %param.5, bf16[2048,1024]{1,0:T(8,128)(2,1)S(1)} %get-tuple-element.12, bf16[2048,1024]{1,0:T(8,128)(2,1)S(1)} %get-tuple-element.11, bf16[4096,1024]{1,0:T(8,128)(2,1)} %collective-permute-done, pred[]{:T(512)S(6)} %eq.14, ...), kind=kOutput, calls=%fused_computation.1 | convolution fusion | flops 34435235840 | bytes 92274688 | tf_op jit(solution)/shard_map/dot_general | solution.py:14
  383.0 690.2 %shard_map.55 = (bf16[2,4,4,512,1024]{4,3,2,1,0:T(8,128)(2,1)}, bf16[2,4,4,1024,512]{4,3,2,1,0:T(8,128)(2,1)}) custom-call(bf16[4096,4096]{1,0:T(8,128)(2,1)} %fusion.schur), custom_call_target="tpu_custom_call" | custom-call | tf_op jit(solution)/shard_map/pallas_call | solution.py:148
  1073.3 167.7 %shard_map.56 = f32[2048,4096]{1,0:T(8,128)} custom-call(s32[2,2048]{1,0:T(2,128)} %bitcast.28, s32[2,2,2048,1]{3,2,1,0:T(8,128)} %copy.10.col_map, bf16[2,4,4,512,1024]{4,3,2,1,0:T(8,128)(2,1)} %get-tuple-element.7.arr_a, bf16[2,4,4,1024,512]{4,3,2,1,0:T(8,128)(2,1)} %get-tuple-element.8.arr_b, bf16[2048,4096]{1,0:T(8,128)(2,1)} %root.1), custom_call_target="tpu_custom_call" | custom-call | tf_op jit(solution)/shard_map/pallas_call | solution.py:261
  (5 shorter events, 0.1 us)
Async XLA Ops:
  6.5 47.1 %all-gather.7.cloned.1.call-start = ((), (), s32[]{:S(2)}) async-start(), calls=%async_computation.1 | async-start | bytes 2621440 | tf_op jit(solution)/shard_map/all_gather | solution.py:293
  7.3 195.3 %all-gather.5.cloned.1.call-start = ((), (), s32[]{:S(2)}) async-start(), calls=%async_computation | async-start | bytes 10485760 | tf_op jit(solution)/shard_map/all_gather | solution.py:292
  223.5 99.8 %copy-start = (s32[2,16384]{1,0:T(2,128)S(1)}, s32[2,16384]{1,0:T(2,128)}, u32[]{:S(2)}) copy-start(s32[2,16384]{1,0:T(2,128)} %param.8) | copy-start | bytes 393220
  223.5 8.0 collective-permute-start.1
  226.3 92.4 %collective-permute-start.2 = (bf16[2048,1024]{1,0:T(8,128)(2,1)}, bf16[2048,1024]{1,0:T(8,128)(2,1)}, u32[]{:S(2)}, u32[]{:S(2)}) collective-permute-start(bf16[2048,1024]{1,0:T(8,128)(2,1)} %get-tuple-element.13), channel_id=1, source_target_pairs={{0,12},{5,13},{10,6},{15,7},{16,28},{21,29},{26,22},{31,23}} | collective-permute-start | bytes 12582920 | tf_op jit(solution)/shard_map/ppermute | solution.py:34
  227.6 107.0 %collective-permute-start = (bf16[4096,1024]{1,0:T(8,128)(2,1)}, bf16[4096,1024]{1,0:T(8,128)(2,1)}, u32[]{:S(2)}, u32[]{:S(2)}) collective-permute-start(bf16[4096,1024]{1,0:T(8,128)(2,1)} %fusion.8), channel_id=1, source_target_pairs={{0,4},{5,1},{10,14},{15,11},{16,20},{21,17},{26,30},{31,27}} | collective-permute-start | bytes 25165832 | tf_op jit(solution)/shard_map/ppermute | solution.py:25
  323.3 7.5 collective-permute-start.3
Sparse Core Ops, SparseCore 0:
  8.9 44.6 all-gather.6
  55.2 147.3 all-gather.4

commit v2 on v1

v2 whole, which is shorter than its diff:
```python
import functools

import jax
import jax.numpy as jnp
from jax import lax
from jax.experimental import pallas as pl
from jax.experimental.pallas import tpu as pltpu
from jax.sharding import PartitionSpec as P

MESH = pl.DeviceIdType.MESH


def contract(left, right):
    return lax.dot_general(
        left, right, (((1,), (1,)), ((), ())), preferred_element_type=jnp.float32
    )


def column_factor(lower, n):
    axes = ("row", "col")
    row_idx = lax.axis_index("row")
    col_idx = lax.axis_index("col")
    half_rows = lower.shape[0] // 2
    top, bottom = lower[:half_rows], lower[half_rows:]
    partner = lax.ppermute(lower, axes, [(c * n + c, (c ^ 1) * n + c) for c in range(n)])
    part = None
    for k in range(1, n // 2):
        evens, odds = [], []
        for c in range(n):
            far = 2 * ((c // 2 + k) % (n // 2))
            evens.append((c * n + c, far * n + c))
            odds.append((c * n + c, (far + 1) * n + c))
        got_even = lax.ppermute(top, axes, evens)
        got_odd = lax.ppermute(bottom, axes, odds)
        got = jnp.where(row_idx % 2 == 0, got_even, got_odd)
        part = got if part is None else part + got
    other = lax.ppermute(part, "row", [(r, r ^ 1) for r in range(n)])
    even = row_idx % 2 == 0
    joined = jnp.concatenate(
        [jnp.where(even, part, other), jnp.where(even, other, part)], axis=0
    )
    near = jnp.where(row_idx == col_idx, lower, partner)
    return jnp.where(row_idx // 2 == col_idx // 2, near, joined)


FLIPS = {
    4: (
        (1, 2, 0), (1, 3, 0), (2, 1, 0), (2, 0, 1), (1, 2, 2), (1, 3, 2),
        (2, 1, 2), (1, 2, 3), (1, 3, 3), (2, 1, 3), (3, 1, 3),
    )
}


def straight(b, c, target_col, n):
    near = jnp.abs(c - target_col) <= jnp.abs(b - target_col)
    for fb, fc, ft in FLIPS.get(n, ()):
        near = near ^ ((b == fb) & (c == fc) & (target_col == ft))
    return near


def exchange_kernel(
    n, row_map, schur, arr_a, arr_b, rowed, square, stage, result,
    send_sem, recv_sem, local_sem, load_sem, store_sem,
):
    total = 2 * n * n
    h = lax.axis_index("half")
    r = lax.axis_index("row")
    z = lax.axis_index("col")
    me = (h * n + r) * n + z
    rs = arr_a.shape[3]
    cs = arr_a.shape[4]
    block = n * rs
    tile = min(256, block)

    def place(index):
        return index // (n * n), (index // n) % n, index % n

    barrier = pltpu.get_barrier_semaphore()

    @pl.loop(1, total)
    def _(step):
        ph, pr, pz = place(lax.rem(me + step, total))
        pl.semaphore_signal(barrier, inc=1, device_id=(ph, pr, pz), device_id_type=MESH)

    pl.semaphore_wait(barrier, total - 1)

    def visit(step, act):
        ph, pr, pz = place(lax.rem(me + step, total))
        t = ph * n + pr
        direct = straight(r, z, pz, n)
        mirror = jnp.logical_not(straight(z, r, pz, n)) & (r != z)
        row_at = pl.multiple_of(t * rs, rs)
        col_at = pl.multiple_of(pz * cs, cs)

        def remote(src, dst, kind):
            act(
                pltpu.make_async_remote_copy(
                    src_ref=src,
                    dst_ref=dst,
                    send_sem=send_sem.at[step, kind],
                    recv_sem=recv_sem.at[h, r, z] if kind == 0 else recv_sem.at[h, z, r],
                    device_id=(ph, pr, pz),
                    device_id_type=MESH,
                )
            )

        for width, fits in ((cs, t > 2 * pz), (rs, t == 2 * pz)):

            @pl.when(fits & direct)
            def _():
                remote(
                    schur.at[pl.ds(row_at, rs), pl.ds(col_at, width)],
                    arr_a.at[h, r, z, :, pl.ds(0, width)],
                    0,
                )

            @pl.when(fits & mirror)
            def _():
                remote(
                    schur.at[pl.ds(col_at, width), pl.ds(row_at, rs)],
                    arr_b.at[h, z, r, pl.ds(0, width), :],
                    1,
                )

    @pl.loop(1, total)
    def _(step):
        visit(step, lambda copy: copy.start())

    my_t = h * n + r
    row_at = pl.multiple_of(my_t * rs, rs)
    col_at = pl.multiple_of(z * cs, cs)
    own_a = pltpu.make_async_copy(
        schur.at[pl.ds(row_at, rs), pl.ds(col_at, cs)], arr_a.at[h, r, z], local_sem.at[0]
    )
    own_b = pltpu.make_async_copy(
        schur.at[pl.ds(col_at, cs), pl.ds(row_at, rs)], arr_b.at[h, z, r], local_sem.at[1]
    )
    own_a.start()
    own_b.start()
    own_a.wait()
    own_b.wait()

    @pl.when(my_t >= 2 * z)
    def _():
        @pl.loop(0, 2 * n)
        def _(k):
            sh = (h + k % 2) % 2
            cc = (z + k // 2) % n

            def moves(b):
                direct = straight(b, cc, z, n)
                into = square.at[pl.ds(b * rs, rs), :]
                load_a = pltpu.make_async_copy(arr_a.at[sh, b, cc], into, load_sem.at[b])
                load_b = pltpu.make_async_copy(
                    arr_b.at[sh, b, cc], stage.at[b], load_sem.at[b]
                )
                return direct, load_a, load_b

            for b in range(n):
                direct, load_a, load_b = moves(b)
                source_row = jnp.where(direct, b, cc)
                source_col = jnp.where(direct, cc, b)
                away = (sh != h) | (source_row != r) | (source_col != z)
                for width, fits in ((cs, my_t > 2 * z), (rs, my_t == 2 * z)):

                    @pl.when(fits & away & direct)
                    def _():
                        dst = arr_a.at[sh, b, cc, :, pl.ds(0, width)]
                        pltpu.make_async_copy(dst, dst, recv_sem.at[sh, b, cc]).wait()

                    @pl.when(fits & away & jnp.logical_not(direct))
                    def _():
                        dst = arr_b.at[sh, b, cc, pl.ds(0, width), :]
                        pltpu.make_async_copy(dst, dst, recv_sem.at[sh, b, cc]).wait()

                @pl.when(direct)
                def _():
                    load_a.start()

                @pl.when(jnp.logical_not(direct))
                def _():
                    load_b.start()

            for b in range(n):
                direct, load_a, load_b = moves(b)

                @pl.when(direct)
                def _():
                    load_a.wait()

                @pl.when(jnp.logical_not(direct))
                def _():
                    load_b.wait()
                    eye = (
                        lax.broadcasted_iota(jnp.int32, (rs, rs), 0)
                        == lax.broadcasted_iota(jnp.int32, (rs, rs), 1)
                    ).astype(jnp.bfloat16)
                    square[pl.ds(b * rs, rs), :] = contract(eye, stage[b]).astype(
                        jnp.bfloat16
                    )

            ids = row_map[pl.ds(sh, 1), :]

            @pl.loop(0, block // tile)
            def _(i):
                at = pl.multiple_of(i * tile, tile)
                pick = (
                    lax.broadcasted_iota(jnp.int32, (tile, block), 0) + at == ids
                ).astype(jnp.bfloat16)
                result[pl.ds(at, tile), :] = jnp.dot(
                    pick, square[...], preferred_element_type=jnp.float32
                ).astype(jnp.bfloat16)

            stores = [
                pltpu.make_async_copy(
                    result.at[:, pl.ds(q * rs, rs)],
                    rowed.at[sh, q, :, pl.ds(pl.multiple_of(cc * rs, rs), rs)],
                    store_sem.at[q],
                )
                for q in range(2)
            ]
            for store in stores:
                store.start()
            for store in stores:
                store.wait()

    @pl.loop(1, total)
    def _(step):
        visit(step, lambda copy: copy.wait_send())


def exchange(row_map, schur, n):
    rs = schur.shape[0] // (2 * n)
    cs = 2 * rs
    block = n * rs
    dtype = schur.dtype
    anywhere = pl.BlockSpec(memory_space=pl.ANY)
    return pl.pallas_call(
        functools.partial(exchange_kernel, n),
        out_shape=(
            jax.ShapeDtypeStruct((2, n, n, rs, cs), dtype),
            jax.ShapeDtypeStruct((2, n, n, cs, rs), dtype),
            jax.ShapeDtypeStruct((2, 2, block, block), dtype),
        ),
        in_specs=[pl.BlockSpec(memory_space=pltpu.VMEM), anywhere],
        out_specs=(anywhere, anywhere, anywhere),
        scratch_shapes=[
            pltpu.VMEM((block, cs), dtype),
            pltpu.VMEM((n, cs, rs), dtype),
            pltpu.VMEM((block, cs), dtype),
            pltpu.SemaphoreType.DMA((2 * n * n, 2)),
            pltpu.SemaphoreType.DMA((2, n, n)),
            pltpu.SemaphoreType.DMA((2,)),
            pltpu.SemaphoreType.DMA((n,)),
            pltpu.SemaphoreType.DMA((2,)),
        ],
        compiler_params=pltpu.CompilerParams(
            collective_id=0, has_side_effects=True, vmem_limit_bytes=48 * 1024 * 1024
        ),
    )(row_map, schur)


def assemble_kernel(n, col_map, rowed, root, out):
    q = pl.program_id(0)
    j = pl.program_id(1)
    t = lax.axis_index("half") * n + lax.axis_index("row")
    c_idx = lax.axis_index("col")
    block = rowed.shape[2]
    tile = min(256, block)
    width = out.shape[1]
    needed = t >= 2 * c_idx + q

    @pl.when(needed)
    def _():
        ids = lax.broadcasted_iota(jnp.int32, (block, width), 1) + j * width
        picks = [
            (col_map[0, h, :, :] == ids).astype(jnp.bfloat16) for h in range(2)
        ]
        first_row = t * block
        first_col = (2 * c_idx + q) * block + j * width
        for i in range(block // tile):
            rows = pl.ds(i * tile, tile)
            value = root[rows, :].astype(jnp.float32)
            for h in range(2):
                value = value + jnp.dot(
                    rowed[h, 0, rows, :], picks[h], preferred_element_type=jnp.float32
                )
            row_ids = lax.broadcasted_iota(jnp.int32, (tile, width), 0) + (
                first_row + i * tile
            )
            col_ids = lax.broadcasted_iota(jnp.int32, (tile, width), 1) + first_col
            out[rows, :] = jnp.where(row_ids >= col_ids, value, 0.0)

    @pl.when(jnp.logical_not(needed))
    def _():
        out[...] = jnp.zeros_like(out)


def assemble(col_map, rowed, root_front, n):
    block = root_front.shape[0]
    width = min(256, block)
    steps = block // width
    return pl.pallas_call(
        functools.partial(assemble_kernel, n),
        grid=(2, steps),
        out_shape=jax.ShapeDtypeStruct(root_front.shape, jnp.float32),
        in_specs=[
            pl.BlockSpec((1, 2, block, 1), lambda q, j: (q, 0, 0, 0)),
            pl.BlockSpec((2, 1, block, block), lambda q, j: (0, q, 0, 0)),
            pl.BlockSpec((block, width), lambda q, j: (0, q * steps + j)),
        ],
        out_specs=pl.BlockSpec((block, width), lambda q, j: (0, q * steps + j)),
        compiler_params=pltpu.CompilerParams(vmem_limit_bytes=58 * 1024 * 1024),
    )(col_map, rowed, root_front)


def body(front, panel, inverse_block, child_maps, root_front):
    n = lax.axis_size("row")
    halves = lax.axis_size("half")
    target = lax.axis_index("half") * n + lax.axis_index("row")
    col_idx = lax.axis_index("col")
    block_front = front[0]
    span = block_front.shape[0]
    share = span // (halves * n)
    block = root_front.shape[0]

    full_panel = lax.all_gather(panel[0], "col", axis=1, tiled=True)
    full_inverse = lax.all_gather(inverse_block[0], "col", axis=1, tiled=True)
    lower_rows = contract(full_panel, full_inverse).astype(jnp.bfloat16)
    lower_cols = column_factor(lower_rows, n)
    update = contract(lower_rows, lower_cols)
    schur_block = (block_front.astype(jnp.float32) - update).astype(jnp.bfloat16)

    runs = child_maps.reshape(halves, n, halves * n, share)

    def local_ids(run):
        picked = lax.dynamic_index_in_dim(runs, run, axis=2, keepdims=False)
        return picked.reshape(halves, n * share) - run * block

    row_map = local_ids(target)
    col_map = jnp.stack([local_ids(2 * col_idx), local_ids(2 * col_idx + 1)])
    rowed = exchange(row_map, schur_block, n)[2]
    return assemble(col_map[..., None], rowed, root_front, n)


def solution(mesh):
    return jax.shard_map(
        body,
        mesh=mesh,
        in_specs=(
            P("half", "row", "col"),
            P("half", "row", "col"),
            P("half", None, "col"),
            P(),
            P(("half", "row"), "col"),
        ),
        out_specs=P(("half", "row"), "col"),
        check_vma=False,
    )
```

time: 1250 us -> 1180 us (0.944)
  Pallas kernels: 858 us -> 791 us
    pallas_call x1, Pallas kernels: 168 us -> 87.1 us  [assemble(): pl.pallas_call(functools.partial(assemble_kernel, n), grid=(2, steps), ou...]
    pallas_call x1, Pallas kernels: 690 us -> 704 us  [exchange(): pl.pallas_call(functools.partial(exchange_kernel, n), out_shape=(jax.Shap...]
where the time goes in v2:
time: 1180 us
  Pallas kernels  791 us (67%)
  waiting for transfers between devices  288 us (24%)
  matrix products  61.7 us (5%)
  between operations  13.5 us (1%)
    pallas_call x1, Pallas kernels, exchange(): pl.pallas_call(functools.partial(exchange_kernel, n), out_shape=(jax.Shap...  704 us
    all_gather x1, waiting for transfers between devices, body(): full_panel = lax.all_gather(panel[0], 'col', axis=1, tiled=True)  149 us
    ppermute x1, waiting for transfers between devices, column_factor(): got_odd = lax.ppermute(bottom, axes, odds)  87.2 us
    pallas_call x1, Pallas kernels, assemble(): pl.pallas_call(functools.partial(assemble_kernel, n), grid=(2, steps), ou...  87.1 us
    dot_general x2, matrix products, contract(): lax.dot_general(left, right, (((1,), (1,)), ((), ())), preferred_element_...  61.7 us
    all_gather x1, waiting for transfers between devices, body(): full_inverse = lax.all_gather(inverse_block[0], 'col', axis=1, tiled=True)  45.6 us
  transfers between devices with their start and end apart: 6, of which 4 were waited for; matrix products, arithmetic and copies ran while one was open for 1% of the time, Pallas kernels for 0%

profile of v2, /device:TPU:11, one launch (start us, length us, event | category | flops | bytes accessed | tf_op | source)
XLA Modules:
  0.0 1180.7 jit_solution(3769793436381426709)
XLA Ops:
  6.5 0.0 all-gather.7.cloned.1.call-start
  6.5 0.7 all-gather.7.cloned.1.call-update
  7.3 0.0 all-gather.5.cloned.1.call-start
  7.3 0.7 all-gather.5.cloned.1.call-update
  8.0 45.6 %all-gather.7.cloned.1.call-done = bf16[1,1024,1024]{2,1,0:T(8,128)(2,1)} async-done(((bf16[1,1024,256]{2,1,0:T(8,128)(2,1)}), bf16[1,1024,1024]{2,1,0:T(8,128)(2,1)}) %all-gather.7.cloned.1.call-update) | async-done | bytes 2097168 | tf_op jit(solution)/shard_map/all_gather | solution.py:328
  53.6 148.9 %all-gather.5.cloned.1.call-done = bf16[1,4096,1024]{2,1,0:T(8,128)(2,1)} async-done(((bf16[1,4096,256]{2,1,0:T(8,128)(2,1)}), bf16[1,4096,1024]{2,1,0:T(8,128)(2,1)}) %all-gather.5.cloned.1.call-update) | async-done | bytes 8388624 | tf_op jit(solution)/shard_map/all_gather | solution.py:327
  202.5 14.9 %fusion.8 = bf16[4096,1024]{1,0:T(8,128)(2,1)} fusion(bf16[1,4096,1024]{2,1,0:T(8,128)(2,1)} %all-gather.5.cloned.1.call-done, bf16[1,1024,1024]{2,1,0:T(8,128)(2,1)} %all-gather.7.cloned.1.call-done), kind=kOutput, calls=%fused_computation.10 | convolution fusion | flops 8594128896 | bytes 18874368 | tf_op jit(solution)/shard_map/dot_general | solution.py:14
  217.5 6.0 fusion.14
  223.5 0.0 copy-start
  223.5 2.8 collective-permute-start.1
  226.3 1.3 collective-permute-start.2
  227.6 3.9 collective-permute-start
  231.5 0.0 collective-permute-done.1
  231.5 87.2 %collective-permute-done.2 = bf16[2048,1024]{1,0:T(8,128)(2,1)} collective-permute-done((bf16[2048,1024]{1,0:T(8,128)(2,1)}, bf16[2048,1024]{1,0:T(8,128)(2,1)}, u32[]{:S(2)}, u32[]{:S(2)}) %collective-permute-start.2) | collective-permute-done | bytes 4194336 | tf_op jit(solution)/shard_map/ppermute | solution.py:34
  318.7 4.6 broadcast_select_fusion.2
  323.3 0.0 collective-permute-start.3
  323.3 0.0 copy-done
  323.4 0.1 subtract_reduce_fusion.1
  323.6 2.6 copy.10.col_map
  326.2 4.6 collective-permute-done.3
  330.8 5.1 broadcast_select_fusion.1
  335.9 0.0 collective-permute-done
  335.9 46.7 %fusion.schur = bf16[4096,4096]{1,0:T(8,128)(2,1)} fusion(bf16[4096,1024]{1,0:T(8,128)(2,1)} %fusion.8, bf16[1,4096,4096]{2,1,0:T(8,128)(2,1)} %param.5, bf16[2048,1024]{1,0:T(8,128)(2,1)} %get-tuple-element.10, bf16[2048,1024]{1,0:T(8,128)(2,1)S(1)} %get-tuple-element.9, bf16[4096,1024]{1,0:T(8,128)(2,1)} %collective-permute-done, pred[]{:T(512)S(6)} %eq.14, ...), kind=kOutput, calls=%fused_computation.1 | convolution fusion | flops 34435235840 | bytes 92274688 | tf_op jit(solution)/shard_map/dot_general | solution.py:14
  382.6 704.1 %shard_map.55 = (bf16[2,4,4,512,1024]{4,3,2,1,0:T(8,128)(2,1)}, bf16[2,4,4,1024,512]{4,3,2,1,0:T(8,128)(2,1)}, bf16[2,2,2048,2048]{3,2,1,0:T(8,128)(2,1)}) custom-call(s32[2,2048]{1,0:T(2,128)S(1)} %bitcast.26, bf16[4096,4096]{1,0:T(8,128)(2,1)} %fusion.schur), custom_call_target="tpu_custom_call" | custom-call | tf_op jit(solution)/shard_map/pallas_call | solution.py:238
  1086.8 87.1 %shard_map.56 = f32[2048,4096]{1,0:T(8,128)} custom-call(s32[2,2,2048,1]{3,2,1,0:T(8,128)} %copy.10.col_map, bf16[2,2,2048,2048]{3,2,1,0:T(8,128)(2,1)} %get-tuple-element.6.rowed, bf16[2048,4096]{1,0:T(8,128)(2,1)} %root.1), custom_call_target="tpu_custom_call" | custom-call | tf_op jit(solution)/shard_map/pallas_call | solution.py:303
  (6 shorter events, 0.1 us)
Async XLA Ops:
  6.5 47.1 %all-gather.7.cloned.1.call-start = ((), (), s32[]{:S(2)}) async-start(), calls=%async_computation.1 | async-start | bytes 2621440 | tf_op jit(solution)/shard_map/all_gather | solution.py:328
  7.3 195.3 %all-gather.5.cloned.1.call-start = ((), (), s32[]{:S(2)}) async-start(), calls=%async_computation | async-start | bytes 10485760 | tf_op jit(solution)/shard_map/all_gather | solution.py:327
  223.5 99.8 %copy-start = (s32[2,16384]{1,0:T(2,128)S(1)}, s32[2,16384]{1,0:T(2,128)}, u32[]{:S(2)}) copy-start(s32[2,16384]{1,0:T(2,128)} %param.8) | copy-start | bytes 393220
  223.5 8.0 collective-permute-start.1
  226.3 92.4 %collective-permute-start.2 = (bf16[2048,1024]{1,0:T(8,128)(2,1)}, bf16[2048,1024]{1,0:T(8,128)(2,1)}, u32[]{:S(2)}, u32[]{:S(2)}) collective-permute-start(bf16[2048,1024]{1,0:T(8,128)(2,1)} %get-tuple-element.11), channel_id=1, source_target_pairs={{0,12},{5,13},{10,6},{15,7},{16,28},{21,29},{26,22},{31,23}} | collective-permute-start | bytes 12582920 | tf_op jit(solution)/shard_map/ppermute | solution.py:34
  227.6 108.3 %collective-permute-start = (bf16[4096,1024]{1,0:T(8,128)(2,1)}, bf16[4096,1024]{1,0:T(8,128)(2,1)}, u32[]{:S(2)}, u32[]{:S(2)}) collective-permute-start(bf16[4096,1024]{1,0:T(8,128)(2,1)} %fusion.8), channel_id=1, source_target_pairs={{0,4},{5,1},{10,14},{15,11},{16,20},{21,17},{26,30},{31,27}} | collective-permute-start | bytes 25165832 | tf_op jit(solution)/shard_map/ppermute | solution.py:25
  323.3 7.5 collective-permute-start.3
Sparse Core Ops, SparseCore 0:
  8.9 44.6 all-gather.6
  55.2 147.3 all-gather.4
